TPU v7x, 512 devices: a whole 4x4x16 slice. The times are simulated.
512 devices in a mesh: dp: 8 (over y_hi, x), mp: 64 (over z, y_lo, core).
Axes of the slice: x: 4, y: 4 (y_hi: 2, y_lo: 2; y = y_hi * 2 + y_lo), z: 16, core: 2. Of those that a mesh axis runs over, the one named last changes fastest.
Arguments:
- activations: bfloat16 [8192, 4096], P(('dp', 'mp')), may hold values from -6 to 6
- out_grads: bfloat16 [8192, 16384], P('dp', 'mp'), may hold values from -0.1875 to 0.1875
- momentum: bfloat16 [8, 4096, 16384], P('dp', None, 'mp'), may hold values from -6 to 6
Outputs:
- remaining: bfloat16 [8, 4096, 16384], P('dp', None, 'mp')
- update: bfloat16 [4096, 16384], P('dp', 'mp')
All inputs are finite; a program needn't handle non-finite values.
Results may differ from a plain program's by a relative error of at most 0.001.
Values may be sent and summed in bfloat16 or wider, within the bound.
A program may use at most 64 MiB of HBM per device.

v0:
```python
import jax
import jax.numpy as jnp
from jax import lax
from jax.sharding import PartitionSpec as P

BETA = 0.9
EPSILON = 1e-06


def low_basis():
    order = jnp.arange(8, dtype=jnp.float32)[:, None]
    position = jnp.arange(64, dtype=jnp.float32)[None, :]
    factor = jnp.where(order == 0, 0.125, 0.17677669529663687).astype(jnp.float32)
    return factor * jnp.cos(jnp.pi * (2.0 * position + 1.0) * order / 128.0)


def forward_low(matrix_in, dct_basis):
    row_count, col_count = matrix_in.shape
    left_part = jnp.einsum(
        "ar,prf->paf",
        dct_basis,
        matrix_in.reshape(row_count // 64, 64, col_count),
        precision=lax.Precision.HIGHEST,
    )
    return jnp.einsum(
        "paqs,bs->paqb",
        left_part.reshape(row_count // 64, 8, col_count // 64, 64),
        dct_basis,
        precision=lax.Precision.HIGHEST,
    )


def inverse_low(low_block, dct_basis):
    band_count, _, span_count, _ = low_block.shape
    right_part = jnp.einsum(
        "paqb,bs->paqs", low_block, dct_basis, precision=lax.Precision.HIGHEST
    ).reshape(band_count, 8, span_count * 64)
    return jnp.einsum(
        "ar,paf->prf", dct_basis, right_part, precision=lax.Precision.HIGHEST
    ).reshape(band_count * 64, span_count * 64)


def soft_sign(matrix_in):
    row_count, col_count = matrix_in.shape
    spans = matrix_in.reshape(row_count // 64, 64, col_count // 64, 64)
    span_power = jnp.mean(spans * spans, axis=(1, 3), keepdims=True)
    return jnp.tanh(spans / jnp.sqrt(span_power + EPSILON)).reshape(row_count, col_count)


def body(activations, out_grads, momentum):
    dct_basis = low_basis()
    local_tokens, row_count = activations.shape
    col_count = out_grads.shape[1]
    band_total = row_count // 64
    gradient = lax.dot_general(
        lax.all_gather(activations, "mp", axis=0, tiled=True),
        out_grads,
        (((0,), (0,)), ((), ())),
        preferred_element_type=jnp.float32,
    )
    old_state = momentum[0].astype(jnp.float32)
    moved = BETA * old_state + gradient
    low_part = forward_low(moved, dct_basis)
    rest = (moved - inverse_low(low_part, dct_basis)).astype(jnp.bfloat16)
    rest, low_block = (rest, low_part)
    remaining = rest[None]
    flat_block = low_block.reshape(band_total, 8, col_count // 64 * 8)
    group_count = lax.axis_size("dp")
    band_rows = band_total // group_count
    gathered = lax.all_gather(flat_block[None], "dp", axis=0, tiled=True)
    summed_all = jnp.sum(gathered, axis=0)
    summed_share = lax.dynamic_slice_in_dim(
        summed_all, lax.axis_index("dp") * band_rows, band_rows, 0
    )
    average = (summed_share / group_count).reshape(band_rows, 8, col_count // 64, 8)
    update = soft_sign(inverse_low(average, dct_basis)).astype(jnp.bfloat16)
    return (remaining, update)


def solution(mesh):
    return jax.shard_map(
        body,
        mesh=mesh,
        in_specs=(P(("dp", "mp"), None), P("dp", "mp"), P("dp", None, "mp")),
        out_specs=(P("dp", None, "mp"), P("dp", "mp")),
        check_vma=False,
    )
```

profile of v0, /device:TPU:1, one launch (start us, length us, event | category | flops | bytes accessed | tf_op | source)
XLA Modules:
  0.0 210.0 jit_solution(791920206411898225)
XLA Ops:
  7.2 0.7 all-gather.2.cloned.1.call-update
  7.9 136.8 %all-gather.2.cloned.1.call-done = bf16[1024,4096]{1,0:T(8,128)(2,1)} async-done(((bf16[16,4096]{1,0:T(8,128)(2,1)}), bf16[1024,4096]{1,0:T(8,128)(2,1)}) %all-gather.2.cloned.1.call-update) | async-done | bytes 8388624 | tf_op jit(solution)/shard_map/all_gather | solution.py:56
  144.8 6.5 %convolution_add_fusion = f32[4096,256]{1,0:T(8,128)S(1)} fusion(bf16[1024,4096]{1,0:T(8,128)(2,1)} %all-gather.2.cloned.1.call-done, bf16[1024,256]{1,0:T(8,128)(2,1)S(1)} %copy-done, bf16[1,4096,256]{2,1,0:T(8,128)(2,1)} %param.5), kind=kOutput, calls=%fused_computation | convolution fusion | flops 2150629376 | bytes 15204352 | tf_op jit(solution)/shard_map/dot_general | solution.py:55
  151.3 1.9 copy-done.1
  153.2 2.3 %convolution_bitcast_fusion = f32[64,8,256]{2,1,0:T(8,128)S(1)} fusion(f32[64,64,256]{2,1,0:T(8,128)S(1)} %bitcast.49, f32[64]{0:T(128)S(1)} %add_multiply_fusion, f32[8]{0:T(128)S(1)} %compare_select_fusion), kind=kOutput, calls=%fused_computation.3 | convolution fusion | flops 100664832 | bytes 4718880 | tf_op jit(solution)/shard_map/ar,prf->paf/dot_general | solution.py:19
  155.5 0.5 reshape.54
  156.0 3.0 %fusion.1 = f32[64,8,4,8]{0,3,2,1:T(8,128)S(1)} fusion(f32[64,8,4,64]{3,2,1,0:T(4,128)S(1)} %reshape.54, f32[64]{0:T(128)S(1)} %add_multiply_fusion, f32[8]{0:T(128)S(1)} %compare_select_fusion), kind=kOutput, calls=%fused_computation.4 | convolution fusion | flops 12584448 | bytes 590112 | tf_op jit(solution)/shard_map/paqs,bs->paqb/dot_general | solution.py:25
  158.9 1.9 fusion.8
  160.8 0.7 copy.29
  161.5 0.6 reshape.55
  162.1 3.8 %fusion.13 = f32[64,256,64]{1,2,0:T(8,128)S(1)} fusion(f32[64,8,256]{2,1,0:T(8,128)S(1)} %reshape.55, f32[64]{0:T(128)S(1)} %add_multiply_fusion, f32[8]{0:T(128)S(1)} %compare_select_fusion), kind=kOutput, calls=%fused_computation.20 | convolution fusion | flops 100664832 | bytes 4718880 | tf_op jit(solution)/shard_map/ar,paf->prf/dot_general | solution.py:38
  165.9 2.5 %fusion = bf16[4096,256]{1,0:T(8,128)(2,1)} fusion(f32[4096,256]{1,0:T(8,128)S(1)} %copy-done.2, f32[64,256,64]{1,2,0:T(8,128)S(1)} %fusion.13), kind=kLoop, calls=%fused_computation.2 | loop fusion | flops 2097152 | bytes 10485760 | tf_op jit(solution)/shard_map/convert_element_type | solution.py:64
  168.3 31.3 %all_gather.7 = f32[8,64,8,32]{1,3,2,0:T(8,128)S(1)} all-gather(f32[1,64,8,32]{1,3,2,0:T(8,128)S(1)} %bitcast.51), channel_id=1, replica_groups=mesh['dp'=8,'mp'=64] {'dp'}, dimensions={0}, use_global_device_ids=true | all-gather | bytes 589824 | tf_op jit(solution)/shard_map/all_gather | solution.py:70
  199.7 0.1 reduce_sum.21
  199.8 0.1 constant_dynamic-slice_fusion
  199.9 0.1 copy.39
  200.0 0.1 reshape.57
  200.1 0.4 fusion.6
  200.5 0.1 reshape.58
  200.6 0.7 fusion.5
  201.4 0.1 reduce_sum.28
  201.5 0.2 div.45
  201.7 0.6 div.46
  202.4 0.8 fusion.4
  (11 shorter events, 0.2 us)
Async XLA Ops:
  7.2 137.6 %copy-start = (bf16[1024,256]{1,0:T(8,128)(2,1)S(1)}, bf16[1024,256]{1,0:T(8,128)(2,1)}, u32[]{:S(2)}) copy-start(bf16[1024,256]{1,0:T(8,128)(2,1)} %param.4) | copy-start | bytes 1572868
  7.2 137.6 %all-gather.2.cloned.1.call-start = ((), (), s32[]{:S(2)}) async-start(), calls=%async_computation | async-start | bytes 8519680 | tf_op jit(solution)/shard_map/all_gather | solution.py:56
  151.3 1.9 copy-start.1
  162.1 3.8 %copy-start.2 = (f32[4096,256]{1,0:T(8,128)S(1)}, f32[4096,256]{1,0:T(8,128)}, u32[]{:S(2)}) copy-start(f32[4096,256]{1,0:T(8,128)} %copy-done.1) | copy-start | bytes 12582916
Sparse Core Ops, SparseCore 0:
  10.2 134.5 all-gather.1
where the time goes:
time: 214 us; the launch traced here: 210 us
  waiting for transfers between devices  138 us (64%)
  blocking collectives  31.3 us (15%)
  matrix products  18.4 us (9%)
  between operations  14.2 us (7%)
  local copies, waits for them, and re-layouts  5.04 us (2%)
  other arithmetic  3.54 us (2%)
    all_gather x1, waiting for transfers between devices, body(): lax.all_gather(activations, 'mp', axis=0, tiled=True)  137 us
    all_gather x1, blocking collectives, body(): gathered = lax.all_gather(flat_block[None], 'dp', axis=0, tiled=True)  31.3 us
    dot_general x1, matrix products, body(): lax.dot_general(lax.all_gather(activations, 'mp', axis=0, tiled=True), ou...  6.52 us
    dot_general x2, matrix products, inverse_low(): jnp.einsum('ar,paf->prf', dct_basis, right_part, precision=lax.Precision....  4.48 us
  transfers between devices with their start and end apart: 1, of which 1 were waited for; matrix products, arithmetic and copies ran while one was open for 0% of the time, Pallas kernels for 0%

commit v1 on v0

v1 whole, which is shorter than its diff:
```python
import functools

import jax
import jax.numpy as jnp
import ml_dtypes
import numpy as np
from jax import lax
from jax.experimental import pallas as pl
from jax.experimental.pallas import tpu as pltpu
from jax.sharding import PartitionSpec as P

BETA = 0.9
EPSILON = 1e-06
MESH = pl.DeviceIdType.MESH
NZ = 16
NB = 5
UP, DOWN = 0, 1
F32, BF16 = jnp.float32, jnp.bfloat16


def low_basis():
    order = np.arange(8)[:, None]
    position = np.arange(64)[None, :]
    factor = np.where(order == 0, 0.125, np.sqrt(2.0 / 64.0))
    return (factor * np.cos(np.pi * (2 * position + 1) * order / 128.0)).astype(np.float32)


def pieces_np(x):
    one = x.astype(ml_dtypes.bfloat16)
    rest = x - one.astype(np.float32)
    two = rest.astype(ml_dtypes.bfloat16)
    three = (rest - two.astype(np.float32)).astype(ml_dtypes.bfloat16)
    return one, two, three


def constants():
    b = low_basis()
    kb = np.kron(np.eye(4, dtype=np.float32), b)
    k1, k2, k3 = pieces_np(kb)
    zero = np.zeros_like(k1)
    first = np.concatenate([np.eye(256, dtype=ml_dtypes.bfloat16), k1, k2, k3], 0)
    wide = [np.tile(k.T, (1, 4)) for k in (k1, k1, k1, k2, k2, k3)]
    to_low = np.concatenate(wide, 0)
    from_low = np.concatenate([k1, k1, k1, k2, k2, k3, zero, zero], 0)
    columns = np.concatenate([k.T for k in (k1, k1, k1, k2, k2, k3)], 1)
    tall = np.concatenate([np.tile(k, (4, 1)) for k in (k1, k1, k1, k2, k2, k3)], 0)
    eight = np.tile(b.T, (4, 1))
    ones = np.kron(np.eye(16, dtype=np.float32), np.ones((8, 8), np.float32)).astype(ml_dtypes.bfloat16)
    return first, to_low, from_low, columns, tall, eight, ones


def pieces(x):
    one = x.astype(BF16)
    rest = x - one.astype(F32)
    two = rest.astype(BF16)
    three = (rest - two.astype(F32)).astype(BF16)
    return one, two, three


def dot(a, b):
    return lax.dot_general(a, b, (((1,), (0,)), ((), ())), preferred_element_type=F32)


def dot_nt(a, b):
    return lax.dot_general(a, b, (((1,), (1,)), ((), ())), preferred_element_type=F32)


def kernel(
    act, grads, mom, c_first, c_to_low, c_from_low, c_columns, c_tall, c_eight, c_ones,
    rem_out, upd_out,
    buf, acc, acc_low, g_in, g_t, m_in, rem, upd, low_out, low_in,
    first, to_low, from_low, columns, tall, eight, ones,
    zr, yr, cr, lr, zs, ys, cs, ls, local, out_sem,
):
    group, lane_id = lax.axis_index("dp"), lax.axis_index("mp")
    z, y, core = lane_id // 4, (lane_id // 2) % 2, lane_id % 2

    def at(zz, yy, cc):
        return {"mp": (zz * 2 + yy) * 2 + cc}

    hop = (at((z + 1) % NZ, y, core), at((z + NZ - 1) % NZ, y, core))
    pair, twin = at(z, 1 - y, core), at(z, y, 1 - core)

    tiles = {"B": (0, NB), "A": (NB, 8 - NB)}
    last = {("B", UP): 8, ("B", DOWN): 7, ("A", UP): 7, ("A", DOWN): 8}
    tall_rows = {"B": 16, "A": 32}
    OWN = 960

    def number(h, kind):
        return h * 2 + (0 if kind == "B" else 1)

    def level(direction, s):
        if isinstance(s, int) and s == 8:
            return 896, 14
        row = (s - 1) * 128 + (64 if direction == DOWN else 0)
        return (row if isinstance(row, int) else pl.multiple_of(row, 64)), (s - 1) * 2 + direction

    def part(h, kind, row, rows):
        begin, count = tiles[kind]
        return buf.at[h, pl.ds(begin, count), pl.ds(row, rows)]

    def remote(src, dst, send, recv, device):
        return pltpu.make_async_remote_copy(
            src_ref=src, dst_ref=dst, send_sem=send, recv_sem=recv, device_id=device, device_id_type=MESH
        )

    def z_copy(h, kind, direction, s):
        n, rows = number(h, kind), tall_rows[kind]
        src = OWN if isinstance(s, int) and s == 1 else level(direction, s - 1)[0]
        dst, _ = level(direction, s)
        return remote(
            part(h, kind, src, rows), part(h, kind, dst, rows),
            zs.at[direction, n], zr.at[direction, n, s - 1], hop[direction],
        )

    def y_copy(h, kind, row, index):
        n = number(h, kind)
        return remote(
            part(h, kind, row, 16), part(h, kind, row + 16, 16), ys.at[n], yr.at[n, index], pair
        )

    def c_copy(h, kind, row, index):
        n = number(h, kind)
        return remote(
            part(h, kind, row, 32), part(h, kind, row + 32, 32), cs.at[n], cr.at[n, index], twin
        )

    def directions(kind, s):
        if not isinstance(s, int):
            return (UP, DOWN)
        return tuple(d for d in (UP, DOWN) if 1 <= s <= last[kind, d])

    def on_z(h, kind, s):
        for direction in directions(kind, s):
            z_copy(h, kind, direction, s).wait_recv()
            if not isinstance(s, int) or s < last[kind, direction]:
                z_copy(h, kind, direction, s + 1).start()
            row, index = level(direction, s)
            (y_copy if kind == "B" else c_copy)(h, kind, row, index).start()

    def on_y(h, s):
        for direction in directions("B", s):
            row, index = level(direction, s)
            y_copy(h, "B", row, index).wait_recv()
            c_copy(h, "B", row, index).start()

    def add_product(h, kind, s):
        for direction in directions(kind, s):
            row, index = level(direction, s)
            c_copy(h, kind, row, index).wait_recv()
        if isinstance(s, int) and s == 8:
            c_copy(h, kind, OWN, 15).wait_recv()
        begin, count = tiles[kind]
        rows = (s - 1) * 128
        rows = rows if isinstance(rows, int) else pl.multiple_of(rows, 128)
        left = g_t[s - 1]

        @pl.loop(begin, begin + count)
        def _(d):
            product = dot(left, buf[h, d, pl.ds(rows, 128), :])
            acc[h, d] += product[:256]
            acc_low[h, d] += product[256:288] + product[288:320] + product[320:352]

    def start_sum(h, kind):
        begin, count = tiles[kind]

        @pl.loop(begin, begin + count)
        def _(d):
            rows = pl.multiple_of(d * 512 + h * 256, 256)
            product = dot_nt(first[...], m_in[pl.ds(rows, 256), :])
            acc[h, d] = BETA * product[:256]
            acc_low[h, d] = BETA * (product[256:288] + product[288:320] + product[320:352])

    lane_group = lax.broadcasted_iota(jnp.int32, (8, 128), 1) // 32

    def by_lanes(a, b, c, d):
        g = lax.broadcasted_iota(jnp.int32, a.shape, 1) // 32
        return jnp.where(g == 0, a, jnp.where(g == 1, b, jnp.where(g == 2, c, d)))

    low_keep = {}

    def low_of(h, kind):
        begin, count = tiles[kind]
        x = acc_low[h, begin : begin + count].reshape(count * 32, 256)
        x1, x2, x3 = pieces(x)
        low = dot(jnp.concatenate([x1, x2, x3, x1, x2, x1], 1), to_low[...])
        low_keep[h, kind] = low
        for i in range(count):
            d = begin + i
            block = [low[i * 32 + 8 * k : i * 32 + 8 * k + 8] for k in range(4)]
            low_out[h, d] = by_lanes(*block)
        for i in range(count):
            d = begin + i
            slot = (group - d + 8) % 8

            @pl.when(d != group)
            def _(d=d, slot=slot):
                remote(low_out.at[h, d], low_in.at[h, slot], ls.at[h], lr.at[h, slot], {"dp": d}).start()

    def remaining_of(h, kind):
        begin, count = tiles[kind]
        l1, l2, l3 = pieces(low_keep[h, kind])
        zero = jnp.zeros_like(l1)
        left = jnp.concatenate([by_lanes(l1, l2, l3, l1), by_lanes(l2, l1, zero, zero)], 1)
        w = dot(left, from_low[...])
        for i in range(count):
            d = begin + i
            w1, w2, w3 = pieces(w[i * 32 : i * 32 + 32])
            expanded = dot(columns[...], jnp.concatenate([w1, w2, w3, w1, w2, w1], 0))
            rest = (acc[h, d] - expanded).T.astype(BF16)
            row = d * 512 + h * 256
            rem[row : row + 256, :] = rest
            pltpu.make_async_copy(
                rem.at[pl.ds(row, 256)], rem_out.at[pl.ds(row, 256)], out_sem.at[0]
            ).start()

    def update_of(h):
        for k in range(1, 8):
            remote(low_out.at[h, 0], low_in.at[h, k], ls.at[h], lr.at[h, k], {"dp": group}).wait_recv()
        total = low_out[h, group]
        for k in range(1, 8):
            total = total + low_in[h, k]
        average = total * 0.125
        square = jnp.sum(average * average, axis=0, keepdims=True)
        s1, s2, s3 = pieces(jnp.broadcast_to(square, (8, 128)))
        power = (dot(s1, ones[...]) + dot(s2, ones[...]) + dot(s3, ones[...])) * (1.0 / 4096.0)
        scaled = average / jnp.sqrt(power + EPSILON)
        spread = jnp.dot(eight[...], scaled, precision=lax.Precision.HIGHEST, preferred_element_type=F32)
        row_group = lax.broadcasted_iota(jnp.int32, (256, 128), 0) // 64
        lanes = lax.broadcasted_iota(jnp.int32, (256, 128), 1) // 32
        spread = jnp.where(row_group == lanes, spread, 0.0)
        s1, s2, s3 = pieces(spread)
        shared = dot(jnp.concatenate([s1, s2, s3, s1, s2, s1], 1), tall[...])
        upd[h * 256 : h * 256 + 256, :] = jnp.tanh(shared).T.astype(BF16)
        pltpu.make_async_copy(
            upd.at[pl.ds(h * 256, 256)], upd_out.at[pl.ds(h * 256, 256)], out_sem.at[1]
        ).start()

    for h in range(2):
        for d in range(8):
            pltpu.make_async_copy(
                act.at[:, pl.ds(d * 512 + h * 256, 256)], buf.at[h, d, pl.ds(OWN, 16)], local.at[0]
            ).start()

    def own_rows(zz, yo, co):
        m = (zz * 2 + (y + yo) % 2) * 2 + (core + co) % 2
        return pl.multiple_of(m * 16, 16)

    for co in range(2):
        for yo in range(2):
            pltpu.make_async_copy(
                grads.at[pl.ds(own_rows(z, yo, co), 16)], g_in.at[pl.ds(OWN + co * 32 + yo * 16, 16)], local.at[1]
            ).start()

            @pl.loop(0, 15)
            def _(k, co=co, yo=yo):
                s = k // 2 + 1
                zz = (z + NZ - s + (k % 2) * 2 * s) % NZ
                row = pl.multiple_of(k * 64 + co * 32 + yo * 16, 16)
                pltpu.make_async_copy(
                    grads.at[pl.ds(own_rows(zz, yo, co), 16)], g_in.at[pl.ds(row, 16)], local.at[1]
                ).start()

    constant = (
        (c_first, first), (c_to_low, to_low), (c_from_low, from_low), (c_columns, columns),
        (c_tall, tall), (c_eight, eight), (c_ones, ones),
    )
    const_copies = [
        pltpu.make_async_copy(src, dst, local.at[3 + i]) for i, (src, dst) in enumerate(constant)
    ]
    for copy in const_copies:
        copy.start()
    pltpu.make_async_copy(mom, m_in, local.at[2]).start()

    barrier = pltpu.get_barrier_semaphore()
    for device in (*hop, pair, twin):
        pl.semaphore_signal(barrier, inc=1, device_id=device, device_id_type=MESH)
    for k in range(1, 8):
        pl.semaphore_signal(barrier, inc=1, device_id={"dp": (group + k) % 8}, device_id_type=MESH)
    pl.semaphore_wait(barrier, 11)

    own_all = buf.at[:, :, pl.ds(OWN, 16)]
    pltpu.make_async_copy(own_all, own_all, local.at[0]).wait()

    y_copy(0, "A", OWN, 15).start()
    y_copy(1, "A", OWN, 15).start()
    for h in range(2):
        for direction in (UP, DOWN):
            z_copy(h, "B", direction, 1).start()
    y_copy(0, "B", OWN, 15).start()
    y_copy(1, "B", OWN, 15).start()

    const_copies[0].wait()
    pltpu.make_async_copy(g_in, g_in, local.at[1]).wait()

    @pl.loop(0, 8)
    def _(s):
        turned = dot_nt(first[...], g_in[pl.ds(pl.multiple_of(s * 128, 128), 128), :])
        g_t[s, :256] = turned[:256].astype(BF16)
        for i, piece in enumerate(pieces(turned[256:288] + turned[288:320] + turned[320:352])):
            g_t[s, 256 + 32 * i : 288 + 32 * i] = piece

    def both_columns(h):
        y_copy(h, "A", OWN, 15).wait_recv()
        for direction in (UP, DOWN):
            z_copy(h, "A", direction, 1).start()
        c_copy(h, "A", OWN, 15).start()

    def own_column(h):
        y_copy(h, "B", OWN, 15).wait_recv()
        c_copy(h, "B", OWN, 15).start()

    both_columns(0)
    pltpu.make_async_copy(m_in, m_in, local.at[2]).wait()
    start_sum(0, "B")
    on_z(0, "B", 1)
    both_columns(1)
    own_column(0)
    own_column(1)
    start_sum(0, "A")
    on_z(1, "B", 1)
    start_sum(1, "B")
    on_z(0, "A", 1)
    on_y(0, 1)
    add_product(0, "A", 1)
    on_z(0, "B", 2)
    start_sum(1, "A")
    on_y(1, 1)
    add_product(0, "B", 1)

    def step(t):
        static = isinstance(t, int)

        def ok(s):
            return not static or 1 <= s <= 8

        on_z(1, "B", t - 1)
        if ok(t - 3):
            add_product(1, "A", t - 3)
        on_z(0, "A", t - 1)
        add_product(1, "B", t - 2)
        on_z(1, "A", t - 2)
        on_y(0, t - 1)
        add_product(0, "A", t - 1)
        if ok(t):
            on_z(0, "B", t)
        on_y(1, t - 1)
        add_product(0, "B", t - 1)

    step(3)

    @pl.loop(4, 7)
    def _(t):
        step(t)

    step(7)
    step(8)
    for copy in const_copies[1:]:
        copy.wait()
    on_z(1, "B", 8)
    add_product(1, "A", 6)
    on_z(0, "A", 8)
    add_product(1, "B", 7)
    on_z(1, "A", 7)
    on_y(0, 8)
    add_product(0, "A", 8)
    low_of(0, "A")
    on_y(1, 8)
    add_product(0, "B", 8)
    low_of(0, "B")
    add_product(1, "A", 7)
    on_z(1, "A", 8)
    remaining_of(0, "A")
    add_product(1, "B", 8)
    low_of(1, "B")
    add_product(1, "A", 8)
    low_of(1, "A")
    remaining_of(0, "B")
    update_of(0)
    remaining_of(1, "B")
    remaining_of(1, "A")
    update_of(1)

    for h in range(2):
        for kind in ("B", "A"):
            n, rows = number(h, kind), tall_rows[kind]
            for direction in (UP, DOWN):
                sent = part(h, kind, 0, rows * last[kind, direction])
                remote(sent, sent, zs.at[direction, n], zr.at[direction, n, 0], hop[direction]).wait_send()
            sent = part(h, kind, 0, 256 if kind == "B" else 16)
            remote(sent, sent, ys.at[n], yr.at[n, 0], pair).wait_send()
            sent = part(h, kind, 0, 512)
            remote(sent, sent, cs.at[n], cr.at[n, 0], twin).wait_send()
        sent = low_out.at[h, pl.ds(0, 7)]
        remote(sent, sent, ls.at[h], lr.at[h, 0], {"dp": group}).wait_send()
    pltpu.make_async_copy(rem, rem_out, out_sem.at[0]).wait()
    pltpu.make_async_copy(upd, upd_out, out_sem.at[1]).wait()


def body(activations, out_grads, momentum):
    consts = [jnp.asarray(c) for c in constants()]
    any_space = pl.BlockSpec(memory_space=pl.ANY)
    dma = pltpu.SemaphoreType.DMA
    remaining, update = pl.pallas_call(
        kernel,
        name="gather_product_low",
        out_shape=(jax.ShapeDtypeStruct((4096, 256), BF16), jax.ShapeDtypeStruct((512, 256), BF16)),
        in_specs=[any_space] * 10,
        out_specs=(any_space, any_space),
        scratch_shapes=[
            pltpu.VMEM((2, 8, 1024, 256), BF16),
            pltpu.VMEM((2, 8, 256, 256), F32),
            pltpu.VMEM((2, 8, 32, 256), F32),
            pltpu.VMEM((1024, 256), BF16),
            pltpu.VMEM((8, 352, 128), BF16),
            pltpu.VMEM((4096, 256), BF16),
            pltpu.VMEM((4096, 256), BF16),
            pltpu.VMEM((512, 256), BF16),
            pltpu.VMEM((2, 8, 8, 128), F32),
            pltpu.VMEM((2, 8, 8, 128), F32),
            *[pltpu.VMEM(c.shape, c.dtype) for c in consts],
            dma((2, 4, 8)),
            dma((4, 16)),
            dma((4, 16)),
            dma((2, 8)),
            dma((2, 4)),
            dma((4,)),
            dma((4,)),
            dma((2,)),
            dma((10,)),
            dma((2,)),
        ],
        compiler_params=pltpu.CompilerParams(
            collective_id=0, has_side_effects=True, vmem_limit_bytes=48 * 1024 * 1024
        ),
        cost_estimate=pl.CostEstimate(flops=2 * 1024 * 4096 * 352, bytes_accessed=5 << 20, transcendentals=512 * 256),
    )(activations, out_grads, momentum[0], *consts)
    return remaining[None], update


def solution(mesh):
    return jax.shard_map(
        body,
        mesh=mesh,
        in_specs=(P(("dp", "mp"), None), P("dp", "mp"), P("dp", None, "mp")),
        out_specs=(P("dp", None, "mp"), P("dp", "mp")),
        check_vma=False,
    )
```

time: 214 us -> 86.9 us (0.41); the launches traced: 210 us -> 86.5 us
  waiting for transfers between devices: 138 us -> 0 us
  Pallas kernels: 0 us -> 75.5 us
  blocking collectives: 31.3 us -> 0 us
  matrix products: 18.4 us -> 0 us
  between operations: 14.2 us -> 0.66 us
  local copies, waits for them, and re-layouts: 5.04 us -> 10.3 us
  other arithmetic: 3.54 us -> 0 us
    all_gather x1 -> x0, waiting for transfers between devices: 137 us -> none  [body(): lax.all_gather(activations, 'mp', axis=0, tiled=True)]
    pallas_call x0 -> x1, Pallas kernels: none -> 75.5 us  [body(): pl.pallas_call(kernel, name='gather_product_low', out_shape=(jax.ShapeDty...]
    all_gather x1 -> x0, blocking collectives: 31.3 us -> none  [body(): gathered = lax.all_gather(flat_block[None], 'dp', axis=0, tiled=True)]
    dot_general x7 -> x0, matrix products: 18.4 us -> none  [the longest x1 6.52 us: body(): lax.dot_general(lax.all_gather(activations, 'mp', axis=0, tiled=True), ou...]
    unnamed x7 -> x20, local copies, waits for them, and re-layouts: 2.03 us -> 10.3 us
    convert_element_type x2 -> x0, other arithmetic: 3.31 us -> none  [the longest x1 2.47 us: body(): rest = (moved - inverse_low(low_part, dct_basis)).astype(jnp.bfloat16)]
  transfers between devices with their start and end apart: 1 -> 0, of which waited for: 1 -> 0; matrix products, arithmetic and copies ran while one was open for 0% -> 0% of each run, Pallas kernels for 0% -> 0%
where the time goes in v1:
time: 86.9 us; the launch traced here: 86.5 us
  Pallas kernels  75.5 us (87%)
  local copies, waits for them, and re-layouts  10.3 us (12%)
    pallas_call x1, Pallas kernels, body(): pl.pallas_call(kernel, name='gather_product_low', out_shape=(jax.ShapeDty...  75.5 us
    unnamed x20, local copies, waits for them, and re-layouts  10.3 us

profile of v1, /device:TPU:1, one launch (start us, length us, event | category | flops | bytes accessed | tf_op | source)
XLA Modules:
  0.0 86.5 jit_solution(4939369453838063652)
XLA Ops:
  0.6 0.0 copy-start
  0.6 1.0 %copy-done = bf16[1024,256]{1,0:T(8,128)(2,1)S(1)} copy-done((bf16[1024,256]{1,0:T(8,128)(2,1)S(1)}, bf16[1024,256]{1,0:T(8,128)(2,1)}, u32[]{:S(2)}) %copy-start) | copy-done | bytes 524312
  1.7 0.0 copy-start.1
  1.7 0.9 %copy-done.1 = bf16[16,4096]{1,0:T(8,128)(2,1)S(1)} copy-done((bf16[16,4096]{1,0:T(8,128)(2,1)S(1)}, bf16[16,4096]{1,0:T(8,128)(2,1)}, u32[]{:S(2)}) %copy-start.1) | copy-done | bytes 131096
  2.6 0.0 copy-start.2
  2.6 1.0 %copy-done.2 = bf16[768,256]{1,0:T(8,128)(2,1)S(1)} copy-done((bf16[768,256]{1,0:T(8,128)(2,1)S(1)}, bf16[768,256]{1,0:T(8,128)(2,1)}, u32[]{:S(2)}) %copy-start.2) | copy-done | bytes 393240
  3.6 0.0 copy-start.3
  3.6 1.0 %copy-done.3 = bf16[1536,128]{1,0:T(8,128)(2,1)S(1)} copy-done((bf16[1536,128]{1,0:T(8,128)(2,1)S(1)}, bf16[1536,128]{1,0:T(8,128)(2,1)}, u32[]{:S(2)}) %copy-start.3) | copy-done | bytes 393240
  4.6 0.0 copy-start.4
  4.6 0.9 %copy-done.4 = bf16[352,256]{1,0:T(8,128)(2,1)S(1)} copy-done((bf16[352,256]{1,0:T(8,128)(2,1)S(1)}, bf16[352,256]{1,0:T(8,128)(2,1)}, u32[]{:S(2)}) %copy-start.4) | copy-done | bytes 180248
  5.5 0.0 copy-start.5
  5.5 0.9 %copy-done.5 = f32[256,8]{1,0:T(8,128)S(1)} copy-done((f32[256,8]{1,0:T(8,128)S(1)}, f32[256,8]{1,0:T(8,128)}, u32[]{:S(2)}) %copy-start.5) | copy-done | bytes 8216
  6.4 0.0 copy-start.6
  6.4 0.9 %copy-done.6 = bf16[256,192]{1,0:T(8,128)(2,1)S(1)} copy-done((bf16[256,192]{1,0:T(8,128)(2,1)S(1)}, bf16[256,192]{1,0:T(8,128)(2,1)}, u32[]{:S(2)}) %copy-start.6) | copy-done | bytes 98328
  7.3 0.0 copy-start.7
  7.3 0.9 %copy-done.7 = bf16[256,256]{1,0:T(8,128)(2,1)S(1)} copy-done((bf16[256,256]{1,0:T(8,128)(2,1)S(1)}, bf16[256,256]{1,0:T(8,128)(2,1)}, u32[]{:S(2)}) %copy-start.7) | copy-done | bytes 131096
  8.2 0.0 copy-start.8
  8.2 0.8 copy-done.8
  9.0 75.5 %gather_product_low.1 = (bf16[4096,256]{1,0:T(8,128)(2,1)S(1)}, bf16[512,256]{1,0:T(8,128)(2,1)S(1)}) custom-call(bf16[16,4096]{1,0:T(8,128)(2,1)S(1)} %copy-done.1, bf16[1024,256]{1,0:T(8,128)(2,1)S(1)} %copy-done, bf16[4096,256]{1,0:T(8,128)(2,1)} %bitcast.3, bf16[352,256]{1,0:T(8,128)(2,1)S(1)} %copy-done.4, bf16[1536,128]{1,0:T(8,128)(2,1)S(1)} %copy-done.3, ...), custom_call_target="tpu_custom_call" | custom-call | flops 2952790016 | bytes 5242880 | tf_op jit(solution)/shard_map/gather_product_low/pallas_call | solution.py:404
  84.5 1.3 %copy.14 = bf16[1,4096,256]{2,1,0:T(8,128)(2,1)} copy(bf16[1,4096,256]{2,1,0:T(8,128)(2,1)S(1)} %bitcast.2) | data formatting | bytes 4194304
  85.8 0.7 copy.15
Async XLA Ops:
  0.6 1.0 %copy-start = (bf16[1024,256]{1,0:T(8,128)(2,1)S(1)}, bf16[1024,256]{1,0:T(8,128)(2,1)}, u32[]{:S(2)}) copy-start(bf16[1024,256]{1,0:T(8,128)(2,1)} %grads.1) | copy-start | bytes 1572868
  1.7 0.9 %copy-start.1 = (bf16[16,4096]{1,0:T(8,128)(2,1)S(1)}, bf16[16,4096]{1,0:T(8,128)(2,1)}, u32[]{:S(2)}) copy-start(bf16[16,4096]{1,0:T(8,128)(2,1)} %act.1) | copy-start | bytes 393220
  2.6 1.0 %copy-start.2 = (bf16[768,256]{1,0:T(8,128)(2,1)S(1)}, bf16[768,256]{1,0:T(8,128)(2,1)}, u32[]{:S(2)}) copy-start(bf16[768,256]{1,0:T(8,128)(2,1)} %constant.18.clone.c_tall) | copy-start | bytes 1179652
  3.6 1.0 %copy-start.3 = (bf16[1536,128]{1,0:T(8,128)(2,1)S(1)}, bf16[1536,128]{1,0:T(8,128)(2,1)}, u32[]{:S(2)}) copy-start(bf16[1536,128]{1,0:T(8,128)(2,1)} %constant.15.clone.c_to_low) | copy-start | bytes 1179652
  4.6 0.9 %copy-start.4 = (bf16[352,256]{1,0:T(8,128)(2,1)S(1)}, bf16[352,256]{1,0:T(8,128)(2,1)}, u32[]{:S(2)}) copy-start(bf16[352,256]{1,0:T(8,128)(2,1)} %constant.14.clone.c_first) | copy-start | bytes 540676
  5.5 0.9 %copy-start.5 = (f32[256,8]{1,0:T(8,128)S(1)}, f32[256,8]{1,0:T(8,128)}, u32[]{:S(2)}) copy-start(f32[256,8]{1,0:T(8,128)} %constant.19.clone.c_eight) | copy-start | bytes 24580
  6.4 0.9 %copy-start.6 = (bf16[256,192]{1,0:T(8,128)(2,1)S(1)}, bf16[256,192]{1,0:T(8,128)(2,1)}, u32[]{:S(2)}) copy-start(bf16[256,192]{1,0:T(8,128)(2,1)} %constant.17.clone.c_columns) | copy-start | bytes 294916
  7.3 0.9 %copy-start.7 = (bf16[256,256]{1,0:T(8,128)(2,1)S(1)}, bf16[256,256]{1,0:T(8,128)(2,1)}, u32[]{:S(2)}) copy-start(bf16[256,256]{1,0:T(8,128)(2,1)} %constant.16.clone.c_from_low) | copy-start | bytes 393220
  8.2 0.8 copy-start.8

commit v2 on v1

--- a/solution.py
+++ b/solution.py
@@ -38,7 +38,7 @@
     kb = np.kron(np.eye(4, dtype=np.float32), b)
     k1, k2, k3 = pieces_np(kb)
     zero = np.zeros_like(k1)
-    first = np.concatenate([np.eye(256, dtype=ml_dtypes.bfloat16), k1, k2, k3], 0)
+    first = np.concatenate([k1, k2, k3], 0)
     wide = [np.tile(k.T, (1, 4)) for k in (k1, k1, k1, k2, k2, k3)]
     to_low = np.concatenate(wide, 0)
     from_low = np.concatenate([k1, k1, k1, k2, k2, k3, zero, zero], 0)
@@ -61,16 +61,12 @@
     return lax.dot_general(a, b, (((1,), (0,)), ((), ())), preferred_element_type=F32)
 
 
-def dot_nt(a, b):
-    return lax.dot_general(a, b, (((1,), (1,)), ((), ())), preferred_element_type=F32)
-
-
 def kernel(
     act, grads, mom, c_first, c_to_low, c_from_low, c_columns, c_tall, c_eight, c_ones,
-    rem_out, upd_out,
-    buf, acc, acc_low, g_in, g_t, m_in, rem, upd, low_out, low_in,
+    rem, upd,
+    buf, acc, acc_low, g_in, g_t, m_in, low_out, low_in,
     first, to_low, from_low, columns, tall, eight, ones,
-    zr, yr, cr, lr, zs, ys, cs, ls, local, out_sem,
+    zr, yr, cr, lr, zs, ys, cs, ls, local,
 ):
     group, lane_id = lax.axis_index("dp"), lax.axis_index("mp")
     z, y, core = lane_id // 4, (lane_id // 2) % 2, lane_id % 2
@@ -138,11 +134,11 @@
             row, index = level(direction, s)
             (y_copy if kind == "B" else c_copy)(h, kind, row, index).start()
 
-    def on_y(h, s):
-        for direction in directions("B", s):
+    def on_y(h, kind, s):
+        for direction in directions(kind, s):
             row, index = level(direction, s)
-            y_copy(h, "B", row, index).wait_recv()
-            c_copy(h, "B", row, index).start()
+            y_copy(h, kind, row, index).wait_recv()
+            c_copy(h, kind, row, index).start()
 
     def add_product(h, kind, s):
         for direction in directions(kind, s):
@@ -155,8 +151,7 @@
         rows = rows if isinstance(rows, int) else pl.multiple_of(rows, 128)
         left = g_t[s - 1]
 
-        @pl.loop(begin, begin + count)
-        def _(d):
+        for d in range(begin, begin + count):
             product = dot(left, buf[h, d, pl.ds(rows, 128), :])
             acc[h, d] += product[:256]
             acc_low[h, d] += product[256:288] + product[288:320] + product[320:352]
@@ -164,14 +159,12 @@
     def start_sum(h, kind):
         begin, count = tiles[kind]
 
-        @pl.loop(begin, begin + count)
-        def _(d):
-            rows = pl.multiple_of(d * 512 + h * 256, 256)
-            product = dot_nt(first[...], m_in[pl.ds(rows, 256), :])
-            acc[h, d] = BETA * product[:256]
-            acc_low[h, d] = BETA * (product[256:288] + product[288:320] + product[320:352])
-
-    lane_group = lax.broadcasted_iota(jnp.int32, (8, 128), 1) // 32
+        for d in range(begin, begin + count):
+            row = d * 512 + h * 256
+            turned = m_in[row : row + 256, :].T
+            acc[h, d] = BETA * turned.astype(F32)
+            product = dot(first[...], turned)
+            acc_low[h, d] = BETA * (product[:32] + product[32:64] + product[64:])
 
     def by_lanes(a, b, c, d):
         g = lax.broadcasted_iota(jnp.int32, a.shape, 1) // 32
@@ -210,9 +203,6 @@
             rest = (acc[h, d] - expanded).T.astype(BF16)
             row = d * 512 + h * 256
             rem[row : row + 256, :] = rest
-            pltpu.make_async_copy(
-                rem.at[pl.ds(row, 256)], rem_out.at[pl.ds(row, 256)], out_sem.at[0]
-            ).start()
 
     def update_of(h):
         for k in range(1, 8):
@@ -232,9 +222,12 @@
         s1, s2, s3 = pieces(spread)
         shared = dot(jnp.concatenate([s1, s2, s3, s1, s2, s1], 1), tall[...])
         upd[h * 256 : h * 256 + 256, :] = jnp.tanh(shared).T.astype(BF16)
-        pltpu.make_async_copy(
-            upd.at[pl.ds(h * 256, 256)], upd_out.at[pl.ds(h * 256, 256)], out_sem.at[1]
-        ).start()
+
+    barrier = pltpu.get_barrier_semaphore()
+    for device in (*hop, pair, twin):
+        pl.semaphore_signal(barrier, inc=1, device_id=device, device_id_type=MESH)
+    for k in range(1, 8):
+        pl.semaphore_signal(barrier, inc=1, device_id={"dp": (group + k) % 8}, device_id_type=MESH)
 
     for h in range(2):
         for d in range(8):
@@ -272,11 +265,6 @@
         copy.start()
     pltpu.make_async_copy(mom, m_in, local.at[2]).start()
 
-    barrier = pltpu.get_barrier_semaphore()
-    for device in (*hop, pair, twin):
-        pl.semaphore_signal(barrier, inc=1, device_id=device, device_id_type=MESH)
-    for k in range(1, 8):
-        pl.semaphore_signal(barrier, inc=1, device_id={"dp": (group + k) % 8}, device_id_type=MESH)
     pl.semaphore_wait(barrier, 11)
 
     own_all = buf.at[:, :, pl.ds(OWN, 16)]
@@ -293,11 +281,11 @@
     const_copies[0].wait()
     pltpu.make_async_copy(g_in, g_in, local.at[1]).wait()
 
-    @pl.loop(0, 8)
-    def _(s):
-        turned = dot_nt(first[...], g_in[pl.ds(pl.multiple_of(s * 128, 128), 128), :])
-        g_t[s, :256] = turned[:256].astype(BF16)
-        for i, piece in enumerate(pieces(turned[256:288] + turned[288:320] + turned[320:352])):
+    for s in range(8):
+        turned = g_in[s * 128 : s * 128 + 128, :].T
+        g_t[s, :256] = turned
+        product = dot(first[...], turned)
+        for i, piece in enumerate(pieces(product[:32] + product[32:64] + product[64:])):
             g_t[s, 256 + 32 * i : 288 + 32 * i] = piece
 
     def both_columns(h):
@@ -310,71 +298,43 @@
         y_copy(h, "B", OWN, 15).wait_recv()
         c_copy(h, "B", OWN, 15).start()
 
+    slot = (
+        (on_z, 1, "A", 2), (add_product, 1, "A", 3), (on_z, 0, "B", 0), (on_y, 0, "B", 1), (add_product, 1, "B", 2),
+        (add_product, 0, "A", 1), (on_z, 1, "B", 0), (on_z, 0, "A", 0), (on_y, 1, "B", 1), (add_product, 0, "B", 1),
+    )
+
+    def run_slot(t):
+        for task, h, kind, lag in slot:
+            if not isinstance(t, int) or 1 <= t - lag <= 8:
+                task(h, kind, t - lag)
+                if task is add_product and isinstance(t, int) and t - lag == 8:
+                    low_of(h, kind)
+
     both_columns(0)
+    run_slot(1)
+    both_columns(1)
     pltpu.make_async_copy(m_in, m_in, local.at[2]).wait()
+    start_sum(0, "A")
     start_sum(0, "B")
-    on_z(0, "B", 1)
-    both_columns(1)
+    run_slot(2)
     own_column(0)
     own_column(1)
-    start_sum(0, "A")
-    on_z(1, "B", 1)
     start_sum(1, "B")
-    on_z(0, "A", 1)
-    on_y(0, 1)
-    add_product(0, "A", 1)
-    on_z(0, "B", 2)
     start_sum(1, "A")
-    on_y(1, 1)
-    add_product(0, "B", 1)
-
-    def step(t):
-        static = isinstance(t, int)
-
-        def ok(s):
-            return not static or 1 <= s <= 8
-
-        on_z(1, "B", t - 1)
-        if ok(t - 3):
-            add_product(1, "A", t - 3)
-        on_z(0, "A", t - 1)
-        add_product(1, "B", t - 2)
-        on_z(1, "A", t - 2)
-        on_y(0, t - 1)
-        add_product(0, "A", t - 1)
-        if ok(t):
-            on_z(0, "B", t)
-        on_y(1, t - 1)
-        add_product(0, "B", t - 1)
-
-    step(3)
+    run_slot(3)
 
     @pl.loop(4, 7)
     def _(t):
-        step(t)
-
-    step(7)
-    step(8)
+        run_slot(t)
+
+    run_slot(7)
+    run_slot(8)
     for copy in const_copies[1:]:
         copy.wait()
-    on_z(1, "B", 8)
-    add_product(1, "A", 6)
-    on_z(0, "A", 8)
-    add_product(1, "B", 7)
-    on_z(1, "A", 7)
-    on_y(0, 8)
-    add_product(0, "A", 8)
-    low_of(0, "A")
-    on_y(1, 8)
-    add_product(0, "B", 8)
-    low_of(0, "B")
-    add_product(1, "A", 7)
-    on_z(1, "A", 8)
+    run_slot(9)
+    run_slot(10)
+    run_slot(11)
     remaining_of(0, "A")
-    add_product(1, "B", 8)
-    low_of(1, "B")
-    add_product(1, "A", 8)
-    low_of(1, "A")
     remaining_of(0, "B")
     update_of(0)
     remaining_of(1, "B")
@@ -393,20 +353,30 @@
             remote(sent, sent, cs.at[n], cr.at[n, 0], twin).wait_send()
         sent = low_out.at[h, pl.ds(0, 7)]
         remote(sent, sent, ls.at[h], lr.at[h, 0], {"dp": group}).wait_send()
-    pltpu.make_async_copy(rem, rem_out, out_sem.at[0]).wait()
-    pltpu.make_async_copy(upd, upd_out, out_sem.at[1]).wait()
+
+
+def store_kernel(rem, upd, rem_out, upd_out, sem):
+    copies = [pltpu.make_async_copy(upd, upd_out, sem.at[0])]
+    for i in range(4):
+        rows = pl.ds(i * 1024, 1024)
+        copies.append(pltpu.make_async_copy(rem.at[rows], rem_out.at[rows], sem.at[1 + i]))
+    for copy in copies:
+        copy.start()
+    for copy in copies:
+        copy.wait()
 
 
 def body(activations, out_grads, momentum):
     consts = [jnp.asarray(c) for c in constants()]
+    shapes = ((4096, 256), (512, 256))
     any_space = pl.BlockSpec(memory_space=pl.ANY)
     dma = pltpu.SemaphoreType.DMA
     remaining, update = pl.pallas_call(
         kernel,
         name="gather_product_low",
-        out_shape=(jax.ShapeDtypeStruct((4096, 256), BF16), jax.ShapeDtypeStruct((512, 256), BF16)),
+        out_shape=tuple(pltpu.VMEM(shape, BF16) for shape in shapes),
         in_specs=[any_space] * 10,
-        out_specs=(any_space, any_space),
+        out_specs=(pl.BlockSpec(memory_space=pltpu.VMEM),) * 2,
         scratch_shapes=[
             pltpu.VMEM((2, 8, 1024, 256), BF16),
             pltpu.VMEM((2, 8, 256, 256), F32),
@@ -414,8 +384,6 @@
             pltpu.VMEM((1024, 256), BF16),
             pltpu.VMEM((8, 352, 128), BF16),
             pltpu.VMEM((4096, 256), BF16),
-            pltpu.VMEM((4096, 256), BF16),
-            pltpu.VMEM((512, 256), BF16),
             pltpu.VMEM((2, 8, 8, 128), F32),
             pltpu.VMEM((2, 8, 8, 128), F32),
             *[pltpu.VMEM(c.shape, c.dtype) for c in consts],
@@ -428,13 +396,20 @@
             dma((4,)),
             dma((2,)),
             dma((10,)),
-            dma((2,)),
         ],
         compiler_params=pltpu.CompilerParams(
-            collective_id=0, has_side_effects=True, vmem_limit_bytes=48 * 1024 * 1024
+            collective_id=0, has_side_effects=True, vmem_limit_bytes=44 * 1024 * 1024
         ),
         cost_estimate=pl.CostEstimate(flops=2 * 1024 * 4096 * 352, bytes_accessed=5 << 20, transcendentals=512 * 256),
-    )(activations, out_grads, momentum[0], *consts)
+    )(*[pltpu.with_memory_space_constraint(x, pltpu.HBM) for x in (activations, out_grads, momentum[0], *consts)])
+    remaining, update = pl.pallas_call(
+        store_kernel,
+        name="store",
+        out_shape=tuple(pltpu.HBM(shape, BF16) for shape in shapes),
+        in_specs=[any_space] * 2,
+        out_specs=(any_space, any_space),
+        scratch_shapes=[dma((5,))],
+    )(*[pltpu.with_memory_space_constraint(x, pltpu.VMEM) for x in (remaining, update)])
     return remaining[None], update
 
 

time: 86.9 us -> 60.9 us (0.70)
  Pallas kernels: 75.5 us -> 60.2 us
  local copies, waits for them, and re-layouts: 10.3 us -> 0 us
    pallas_call x1 -> x2, Pallas kernels: 75.5 us -> 60.2 us  [the longest x1 58.7 us: body(): pl.pallas_call(kernel, name='gather_product_low', out_shape=tuple((pltpu....]
    unnamed x20 -> x0, local copies, waits for them, and re-layouts: 10.3 us -> none
where the time goes in v2:
time: 60.9 us; the launch traced here: 60.8 us
  Pallas kernels  60.2 us (99%)
  between operations  0.64 us (1%)
    pallas_call x1, Pallas kernels, body(): pl.pallas_call(kernel, name='gather_product_low', out_shape=tuple((pltpu....  58.7 us
    pallas_call x1, Pallas kernels, body(): pl.pallas_call(store_kernel, name='store', out_shape=tuple((pltpu.HBM(sha...  1.44 us

profile of v2, /device:TPU:1, one launch (start us, length us, event | category | flops | bytes accessed | tf_op | source)
XLA Modules:
  0.0 60.8 jit_solution(7097940675130861090)
XLA Ops:
  0.6 58.7 %gather_product_low.1 = (bf16[4096,256]{1,0:T(8,128)(2,1)S(1)}, bf16[512,256]{1,0:T(8,128)(2,1)S(1)}) custom-call(bf16[16,4096]{1,0:T(8,128)(2,1)} %act.1, bf16[1024,256]{1,0:T(8,128)(2,1)} %grads.1, bf16[4096,256]{1,0:T(8,128)(2,1)} %bitcast.2, bf16[96,256]{1,0:T(8,128)(2,1)} %constant.14.clone.c_first, bf16[1536,128]{1,0:T(8,128)(2,1)} %constant.15.clone.c_to_low, ...), custom_call_target="tpu_custom_call" | custom-call | flops 2952790016 | bytes 5242880 | tf_op jit(solution)/shard_map/gather_product_low/pallas_call | solution.py:374
  59.4 1.4 %store.1 = (bf16[4096,256]{1,0:T(8,128)(2,1)}, bf16[512,256]{1,0:T(8,128)(2,1)}) custom-call(bf16[4096,256]{1,0:T(8,128)(2,1)S(1)} %get-tuple-element.6.rem, bf16[512,256]{1,0:T(8,128)(2,1)S(1)} %get-tuple-element.7.upd), custom_call_target="tpu_custom_call" | custom-call | tf_op jit(solution)/shard_map/store/pallas_call | solution.py:405

commit v3 on v2

--- a/solution.py
+++ b/solution.py
@@ -61,11 +61,25 @@
     return lax.dot_general(a, b, (((1,), (0,)), ((), ())), preferred_element_type=F32)
 
 
+def update_rows(average, eight, ones, tall):
+    square = jnp.sum(average * average, axis=0, keepdims=True)
+    s1, s2, s3 = pieces(jnp.broadcast_to(square, (8, 128)))
+    power = (dot(s1, ones[...]) + dot(s2, ones[...]) + dot(s3, ones[...])) * (1.0 / 4096.0)
+    scaled = average / jnp.sqrt(power + EPSILON)
+    spread = jnp.dot(eight[...], scaled, precision=lax.Precision.HIGHEST, preferred_element_type=F32)
+    row_group = lax.broadcasted_iota(jnp.int32, (256, 128), 0) // 64
+    lanes = lax.broadcasted_iota(jnp.int32, (256, 128), 1) // 32
+    spread = jnp.where(row_group == lanes, spread, 0.0)
+    s1, s2, s3 = pieces(spread)
+    shared = dot(jnp.concatenate([s1, s2, s3, s1, s2, s1], 1), tall[...])
+    return jnp.tanh(shared).T.astype(BF16)
+
+
 def kernel(
     act, grads, mom, c_first, c_to_low, c_from_low, c_columns, c_tall, c_eight, c_ones,
-    rem, upd,
+    rem, upd, average, tall, eight, ones,
     buf, acc, acc_low, g_in, g_t, m_in, low_out, low_in,
-    first, to_low, from_low, columns, tall, eight, ones,
+    first, to_low, from_low, columns,
     zr, yr, cr, lr, zs, ys, cs, ls, local,
 ):
     group, lane_id = lax.axis_index("dp"), lax.axis_index("mp")
@@ -204,24 +218,13 @@
             row = d * 512 + h * 256
             rem[row : row + 256, :] = rest
 
-    def update_of(h):
+    def average_of(h):
         for k in range(1, 8):
             remote(low_out.at[h, 0], low_in.at[h, k], ls.at[h], lr.at[h, k], {"dp": group}).wait_recv()
         total = low_out[h, group]
         for k in range(1, 8):
             total = total + low_in[h, k]
-        average = total * 0.125
-        square = jnp.sum(average * average, axis=0, keepdims=True)
-        s1, s2, s3 = pieces(jnp.broadcast_to(square, (8, 128)))
-        power = (dot(s1, ones[...]) + dot(s2, ones[...]) + dot(s3, ones[...])) * (1.0 / 4096.0)
-        scaled = average / jnp.sqrt(power + EPSILON)
-        spread = jnp.dot(eight[...], scaled, precision=lax.Precision.HIGHEST, preferred_element_type=F32)
-        row_group = lax.broadcasted_iota(jnp.int32, (256, 128), 0) // 64
-        lanes = lax.broadcasted_iota(jnp.int32, (256, 128), 1) // 32
-        spread = jnp.where(row_group == lanes, spread, 0.0)
-        s1, s2, s3 = pieces(spread)
-        shared = dot(jnp.concatenate([s1, s2, s3, s1, s2, s1], 1), tall[...])
-        upd[h * 256 : h * 256 + 256, :] = jnp.tanh(shared).T.astype(BF16)
+        return total * 0.125
 
     barrier = pltpu.get_barrier_semaphore()
     for device in (*hop, pair, twin):
@@ -234,6 +237,19 @@
             pltpu.make_async_copy(
                 act.at[:, pl.ds(d * 512 + h * 256, 256)], buf.at[h, d, pl.ds(OWN, 16)], local.at[0]
             ).start()
+
+    pl.semaphore_wait(barrier, 11)
+
+    own_all = buf.at[:, :, pl.ds(OWN, 16)]
+    pltpu.make_async_copy(own_all, own_all, local.at[0]).wait()
+
+    y_copy(0, "A", OWN, 15).start()
+    y_copy(1, "A", OWN, 15).start()
+    for h in range(2):
+        for direction in (UP, DOWN):
+            z_copy(h, "B", direction, 1).start()
+    y_copy(0, "B", OWN, 15).start()
+    y_copy(1, "B", OWN, 15).start()
 
     def own_rows(zz, yo, co):
         m = (zz * 2 + (y + yo) % 2) * 2 + (core + co) % 2
@@ -265,18 +281,31 @@
         copy.start()
     pltpu.make_async_copy(mom, m_in, local.at[2]).start()
 
-    pl.semaphore_wait(barrier, 11)
-
-    own_all = buf.at[:, :, pl.ds(OWN, 16)]
-    pltpu.make_async_copy(own_all, own_all, local.at[0]).wait()
-
-    y_copy(0, "A", OWN, 15).start()
-    y_copy(1, "A", OWN, 15).start()
-    for h in range(2):
+    def both_columns(h):
+        y_copy(h, "A", OWN, 15).wait_recv()
         for direction in (UP, DOWN):
-            z_copy(h, "B", direction, 1).start()
-    y_copy(0, "B", OWN, 15).start()
-    y_copy(1, "B", OWN, 15).start()
+            z_copy(h, "A", direction, 1).start()
+        c_copy(h, "A", OWN, 15).start()
+
+    def own_column(h):
+        y_copy(h, "B", OWN, 15).wait_recv()
+        c_copy(h, "B", OWN, 15).start()
+
+    slot = (
+        (on_z, 1, "A", 2), (add_product, 1, "A", 3), (on_z, 0, "B", 0), (on_y, 0, "B", 1), (add_product, 1, "B", 2),
+        (add_product, 0, "A", 1), (on_z, 1, "B", 0), (on_z, 0, "A", 0), (on_y, 1, "B", 1), (add_product, 0, "B", 1),
+    )
+
+    def run_slot(t):
+        for task, h, kind, lag in slot:
+            if not isinstance(t, int) or 1 <= t - lag <= 8:
+                task(h, kind, t - lag)
+                if task is add_product and isinstance(t, int) and t - lag == 8:
+                    low_of(h, kind)
+
+    both_columns(0)
+    run_slot(1)
+    both_columns(1)
 
     const_copies[0].wait()
     pltpu.make_async_copy(g_in, g_in, local.at[1]).wait()
@@ -288,31 +317,6 @@
         for i, piece in enumerate(pieces(product[:32] + product[32:64] + product[64:])):
             g_t[s, 256 + 32 * i : 288 + 32 * i] = piece
 
-    def both_columns(h):
-        y_copy(h, "A", OWN, 15).wait_recv()
-        for direction in (UP, DOWN):
-            z_copy(h, "A", direction, 1).start()
-        c_copy(h, "A", OWN, 15).start()
-
-    def own_column(h):
-        y_copy(h, "B", OWN, 15).wait_recv()
-        c_copy(h, "B", OWN, 15).start()
-
-    slot = (
-        (on_z, 1, "A", 2), (add_product, 1, "A", 3), (on_z, 0, "B", 0), (on_y, 0, "B", 1), (add_product, 1, "B", 2),
-        (add_product, 0, "A", 1), (on_z, 1, "B", 0), (on_z, 0, "A", 0), (on_y, 1, "B", 1), (add_product, 0, "B", 1),
-    )
-
-    def run_slot(t):
-        for task, h, kind, lag in slot:
-            if not isinstance(t, int) or 1 <= t - lag <= 8:
-                task(h, kind, t - lag)
-                if task is add_product and isinstance(t, int) and t - lag == 8:
-                    low_of(h, kind)
-
-    both_columns(0)
-    run_slot(1)
-    both_columns(1)
     pltpu.make_async_copy(m_in, m_in, local.at[2]).wait()
     start_sum(0, "A")
     start_sum(0, "B")
@@ -336,10 +340,10 @@
     run_slot(11)
     remaining_of(0, "A")
     remaining_of(0, "B")
-    update_of(0)
+    upd[...] = update_rows(average_of(0), eight, ones, tall)
     remaining_of(1, "B")
     remaining_of(1, "A")
-    update_of(1)
+    average[...] = average_of(1)
 
     for h in range(2):
         for kind in ("B", "A"):
@@ -355,28 +359,32 @@
         remote(sent, sent, ls.at[h], lr.at[h, 0], {"dp": group}).wait_send()
 
 
-def store_kernel(rem, upd, rem_out, upd_out, sem):
-    copies = [pltpu.make_async_copy(upd, upd_out, sem.at[0])]
+def store_kernel(rem, upd, average, tall, eight, ones, rem_out, upd_out, later, sem):
+    copies = [pltpu.make_async_copy(upd, upd_out.at[pl.ds(0, 256)], sem.at[0])]
     for i in range(4):
         rows = pl.ds(i * 1024, 1024)
-        copies.append(pltpu.make_async_copy(rem.at[rows], rem_out.at[rows], sem.at[1 + i]))
+        copies.append(pltpu.make_async_copy(rem.at[rows], rem_out.at[rows], sem.at[2 + i]))
     for copy in copies:
         copy.start()
+    later[...] = update_rows(average[...], eight, ones, tall)
+    copies.append(pltpu.make_async_copy(later, upd_out.at[pl.ds(256, 256)], sem.at[1]))
+    copies[-1].start()
     for copy in copies:
         copy.wait()
 
 
 def body(activations, out_grads, momentum):
     consts = [jnp.asarray(c) for c in constants()]
-    shapes = ((4096, 256), (512, 256))
+    kept = (((4096, 256), BF16), ((256, 256), BF16), ((8, 128), F32)) + tuple((c.shape, c.dtype) for c in consts[4:])
     any_space = pl.BlockSpec(memory_space=pl.ANY)
+    vmem_space = pl.BlockSpec(memory_space=pltpu.VMEM)
     dma = pltpu.SemaphoreType.DMA
-    remaining, update = pl.pallas_call(
+    results = pl.pallas_call(
         kernel,
         name="gather_product_low",
-        out_shape=tuple(pltpu.VMEM(shape, BF16) for shape in shapes),
+        out_shape=tuple(pltpu.VMEM(shape, dtype) for shape, dtype in kept),
         in_specs=[any_space] * 10,
-        out_specs=(pl.BlockSpec(memory_space=pltpu.VMEM),) * 2,
+        out_specs=(vmem_space,) * 6,
         scratch_shapes=[
             pltpu.VMEM((2, 8, 1024, 256), BF16),
             pltpu.VMEM((2, 8, 256, 256), F32),
@@ -386,7 +394,7 @@
             pltpu.VMEM((4096, 256), BF16),
             pltpu.VMEM((2, 8, 8, 128), F32),
             pltpu.VMEM((2, 8, 8, 128), F32),
-            *[pltpu.VMEM(c.shape, c.dtype) for c in consts],
+            *[pltpu.VMEM(c.shape, c.dtype) for c in consts[:4]],
             dma((2, 4, 8)),
             dma((4, 16)),
             dma((4, 16)),
@@ -405,11 +413,11 @@
     remaining, update = pl.pallas_call(
         store_kernel,
         name="store",
-        out_shape=tuple(pltpu.HBM(shape, BF16) for shape in shapes),
-        in_specs=[any_space] * 2,
+        out_shape=(pltpu.HBM((4096, 256), BF16), pltpu.HBM((512, 256), BF16)),
+        in_specs=[vmem_space] * 6,
         out_specs=(any_space, any_space),
-        scratch_shapes=[dma((5,))],
-    )(*[pltpu.with_memory_space_constraint(x, pltpu.VMEM) for x in (remaining, update)])
+        scratch_shapes=[pltpu.VMEM((256, 256), BF16), dma((6,))],
+    )(*[pltpu.with_memory_space_constraint(x, pltpu.VMEM) for x in results])
     return remaining[None], update
 
 

time: 60.9 us -> 60.2 us (0.989)
  Pallas kernels: 60.2 us -> 59.4 us
    pallas_call x1, Pallas kernels: 58.7 us -> 57.9 us  [body(): pl.pallas_call(kernel, name='gather_product_low', out_shape=tuple((pltpu....]
where the time goes in v3:
time: 60.2 us; the launch traced here: 60 us
  Pallas kernels  59.4 us (99%)
  between operations  0.64 us (1%)
    pallas_call x1, Pallas kernels, body(): pl.pallas_call(kernel, name='gather_product_low', out_shape=tuple((pltpu....  57.9 us
    pallas_call x1, Pallas kernels, body(): pl.pallas_call(store_kernel, name='store', out_shape=(pltpu.HBM((4096, 25...  1.55 us

profile of v3, /device:TPU:1, one launch (start us, length us, event | category | flops | bytes accessed | tf_op | source)
XLA Modules:
  0.0 60.0 jit_solution(7625174257655691306)
XLA Ops:
  0.6 57.9 %gather_product_low.1 = (bf16[4096,256]{1,0:T(8,128)(2,1)S(1)}, bf16[256,256]{1,0:T(8,128)(2,1)S(1)}, f32[8,128]{1,0:T(8,128)S(1)}, bf16[768,256]{1,0:T(8,128)(2...) custom-call(bf16[16,4096]{1,0:T(8,128)(2,1)} %act.1, bf16[1024,256]{1,0:T(8,128)(2,1)} %grads.1, ...), custom_call_target="tpu_custom_call" | custom-call | flops 2952790016 | bytes 5242880 | tf_op jit(solution)/shard_map/gather_product_low/pallas_call | solution.py:382
  58.5 1.6 %store.1 = (bf16[4096,256]{1,0:T(8,128)(2,1)}, bf16[512,256]{1,0:T(8,128)(2,1)}) custom-call(bf16[4096,256]{1,0:T(8,128)(2,1)S(1)} %get-tuple-element.10.rem, bf16[256,256]{1,0:T(8,128)(2,1)S(1)} %get-tuple-element.11.upd, f32[8,128]{1,0:T(8,128)S(1)} %get-tuple-element.12.average, bf16[768,256]{1,0:T(8,128)(2,1)S(1)} %get-tuple-element.13.tall, ...), custom_call_target="tpu_custom_call" | custom-call | tf_op jit(solution)/shard_map/store/pallas_call | solution.py:413

commit v4 on v3

--- a/solution.py
+++ b/solution.py
@@ -80,7 +80,7 @@
     rem, upd, average, tall, eight, ones,
     buf, acc, acc_low, g_in, g_t, m_in, low_out, low_in,
     first, to_low, from_low, columns,
-    zr, yr, cr, lr, zs, ys, cs, ls, local,
+    zr, yr, cr, lr, zs, ys, cs, ls, local, met, met_all,
 ):
     group, lane_id = lax.axis_index("dp"), lax.axis_index("mp")
     z, y, core = lane_id // 4, (lane_id // 2) % 2, lane_id % 2
@@ -229,8 +229,10 @@
     barrier = pltpu.get_barrier_semaphore()
     for device in (*hop, pair, twin):
         pl.semaphore_signal(barrier, inc=1, device_id=device, device_id_type=MESH)
-    for k in range(1, 8):
-        pl.semaphore_signal(barrier, inc=1, device_id={"dp": (group + k) % 8}, device_id_type=MESH)
+    row_start = (group // 4) * 4
+    near = ({"dp": row_start + (group + 1) % 4}, {"dp": row_start + (group + 3) % 4}, {"dp": (group + 4) % 8})
+    for device in near:
+        pl.semaphore_signal(barrier, inc=1, device_id=device, device_id_type=MESH)
 
     for h in range(2):
         for d in range(8):
@@ -238,7 +240,7 @@
                 act.at[:, pl.ds(d * 512 + h * 256, 256)], buf.at[h, d, pl.ds(OWN, 16)], local.at[0]
             ).start()
 
-    pl.semaphore_wait(barrier, 11)
+    pl.semaphore_wait(barrier, 7)
 
     own_all = buf.at[:, :, pl.ds(OWN, 16)]
     pltpu.make_async_copy(own_all, own_all, local.at[0]).wait()
@@ -320,6 +322,8 @@
     pltpu.make_async_copy(m_in, m_in, local.at[2]).wait()
     start_sum(0, "A")
     start_sum(0, "B")
+    for device in near:
+        pl.semaphore_signal(met, inc=1, device_id=device, device_id_type=MESH)
     run_slot(2)
     own_column(0)
     own_column(1)
@@ -331,8 +335,11 @@
     def _(t):
         run_slot(t)
 
+    pl.semaphore_wait(met, 3)
+    pl.semaphore_signal(met_all, inc=1, device_id=near[2], device_id_type=MESH)
     run_slot(7)
     run_slot(8)
+    pl.semaphore_wait(met_all, 1)
     for copy in const_copies[1:]:
         copy.wait()
     run_slot(9)
@@ -404,6 +411,8 @@
             dma((4,)),
             dma((2,)),
             dma((10,)),
+            pltpu.SemaphoreType.REGULAR,
+            pltpu.SemaphoreType.REGULAR,
         ],
         compiler_params=pltpu.CompilerParams(
             collective_id=0, has_side_effects=True, vmem_limit_bytes=44 * 1024 * 1024

time: 60.2 us -> 59.6 us (0.990)
  no operation moved by 1% of the time
where the time goes in v4:
time: 59.6 us; the launch traced here: 59.5 us
  Pallas kernels  58.8 us (99%)
  between operations  0.64 us (1%)
    pallas_call x1, Pallas kernels, body(): pl.pallas_call(kernel, name='gather_product_low', out_shape=tuple((pltpu....  57.3 us
    pallas_call x1, Pallas kernels, body(): pl.pallas_call(store_kernel, name='store', out_shape=(pltpu.HBM((4096, 25...  1.55 us

profile of v4, /device:TPU:1, one launch (start us, length us, event | category | flops | bytes accessed | tf_op | source)
XLA Modules:
  0.0 59.5 jit_solution(7878971864027353153)
XLA Ops:
  0.6 57.3 %gather_product_low.1 = (bf16[4096,256]{1,0:T(8,128)(2,1)S(1)}, bf16[256,256]{1,0:T(8,128)(2,1)S(1)}, f32[8,128]{1,0:T(8,128)S(1)}, bf16[768,256]{1,0:T(8,128)(2...) custom-call(bf16[16,4096]{1,0:T(8,128)(2,1)} %act.1, bf16[1024,256]{1,0:T(8,128)(2,1)} %grads.1, ...), custom_call_target="tpu_custom_call" | custom-call | flops 2952790016 | bytes 5242880 | tf_op jit(solution)/shard_map/gather_product_low/pallas_call | solution.py:389
  57.9 1.6 %store.1 = (bf16[4096,256]{1,0:T(8,128)(2,1)}, bf16[512,256]{1,0:T(8,128)(2,1)}) custom-call(bf16[4096,256]{1,0:T(8,128)(2,1)S(1)} %get-tuple-element.10.rem, bf16[256,256]{1,0:T(8,128)(2,1)S(1)} %get-tuple-element.11.upd, f32[8,128]{1,0:T(8,128)S(1)} %get-tuple-element.12.average, bf16[768,256]{1,0:T(8,128)(2,1)S(1)} %get-tuple-element.13.tall, ...), custom_call_target="tpu_custom_call" | custom-call | tf_op jit(solution)/shard_map/store/pallas_call | solution.py:422
